TPU v7x, 512 devices: a whole 4x8x8 slice. The times are simulated.
512 devices in a mesh: layer: 4 (over y_lo, core), dp: 128 (over z, x, y_hi).
Axes of the slice: x: 4, y: 8 (y_hi: 4, y_lo: 2; y = y_hi * 2 + y_lo), z: 8, core: 2. Of those that a mesh axis runs over, the one named last changes fastest.
Arguments:
- activations: bfloat16 [4, 16384, 5120], P('layer', 'dp'), may hold values from -6 to 6
- out_grads: bfloat16 [4, 16384, 5120], P('layer', 'dp'), may hold values from -6 to 6
- projectors: bfloat16 [4, 5120, 128], P('layer'), may hold values from -0.078125 to 0.078125
- rewards: float32 [512], P('dp'), may hold values from -8 to 8
- lengths: int32 [512], P('dp'), may hold values from 1 to 32, 12288 in all
- pairing: int32 [256, 2], P('dp'), may hold values from 0 to 3, as said below
- queries: bfloat16 [4, 1024, 4096], P('layer', 'dp'), may hold values from -0.0078125 to 0.0078125
Outputs:
- scores: float32 [256, 1024], P('dp', 'layer')
Inputs may be any that keep to these rules, and one draw needn't show every extreme that they name: `pairing`: the 2 pairs of one dp index name each of that index's 2 * 2 sequences exactly once.
All inputs are finite; a program needn't handle non-finite values. No bound on the sum of `lengths` on one device may be relied on, other than what follows from the above.
Results may differ from a plain program's by a relative error of at most 0.0029.
Values may be sent and summed in bfloat16 or wider, within the bound.
No kernel may reach another device: no remote copies, remote signals or barrier semaphores. Data moves between devices by JAX's collectives and lax.ppermute only.
A program may use at most 64 MiB of HBM per device.

v0:
```python
import jax
import jax.numpy as jnp
from jax import lax
from jax.sharding import PartitionSpec as P


def local(activations, out_grads, projectors, rewards, lengths, pairing, queries):
    half = projectors.shape[2] // 2
    seq_count = lengths.shape[0]
    seq_len = activations.shape[1] // seq_count
    proj_act = jnp.dot(activations[0], projectors[0, :, :half], preferred_element_type=jnp.float32)
    proj_grad = jnp.dot(out_grads[0], projectors[0, :, half:], preferred_element_type=jnp.float32)
    places = jnp.arange(seq_len, dtype=jnp.int32)
    live_mask = (places[None, :] < lengths[:, None]).astype(jnp.float32)
    grad_seq = proj_grad.reshape(seq_count, seq_len, half) * live_mask[:, :, None]
    act_seq = proj_act.reshape(seq_count, seq_len, half)
    seq_grads = jnp.einsum(
        "stk,stj->skj", grad_seq, act_seq, precision=lax.Precision.HIGHEST
    ).reshape(seq_count, half * half)
    chosen = pairing[:, 0]
    rejected = pairing[:, 1]
    margin_weight = 1.0 - jax.nn.sigmoid(rewards[chosen] - rewards[rejected])
    train_grads = (margin_weight[:, None] * (seq_grads[rejected] - seq_grads[chosen])).astype(
        jnp.bfloat16
    )
    partial_scores = jnp.dot(
        train_grads,
        lax.all_gather(queries, "dp", axis=1, tiled=True)[0].T,
        preferred_element_type=jnp.float32,
    )
    return lax.psum_scatter(partial_scores, "layer", scatter_dimension=1, tiled=True)


def solution(mesh):
    return jax.shard_map(
        local,
        mesh=mesh,
        in_specs=(
            P("layer", "dp", None),
            P("layer", "dp", None),
            P("layer", None, None),
            P("dp"),
            P("dp"),
            P("dp", None),
            P("layer", "dp", None),
        ),
        out_specs=P("dp", "layer"),
        check_vma=False,
    )
```

profile of v0, /device:TPU:1, one launch (start us, length us, event | category | flops | bytes accessed | tf_op | source)
XLA Modules:
  0.0 206.6 jit_solution(4026747524482920533)
XLA Ops:
  6.5 0.0 copy-start
  6.5 0.0 all-gather.2.cloned.1.call-start
  6.5 0.7 all-gather.2.cloned.1.call-update
  7.3 0.0 reduce-scatter.4.cloned.1.call-start
  7.3 1.0 fusion.15
  8.3 1.3 gather_fusion.1
  9.6 1.3 gather_fusion
  10.9 0.7 fusion.14
  11.6 0.0 copy-done
  11.6 0.0 copy-start.1
  11.6 0.0 copy-start.2
  11.6 2.0 fusion.2
  13.6 0.0 copy-done.1
  13.6 0.1 copy-done.2
  13.7 0.7 fusion.11
  14.4 0.4 fusion.17
  14.8 0.1 reshape.41
  14.9 0.6 gather_fusion.3
  15.5 0.6 gather_fusion.2
  16.1 155.1 %all-gather.2.cloned.1.call-done = bf16[1,1024,4096]{2,1,0:T(8,128)(2,1)} async-done(((bf16[1,8,4096]{2,1,0:T(8,128)(2,1)}), bf16[1,1024,4096]{2,1,0:T(8,128)(2,1)}) %all-gather.2.cloned.1.call-update) | async-done | bytes 8388624 | tf_op jit(solution)/shard_map/all_gather | solution.py:28
  171.2 6.6 %fusion.8 = f32[1024,2]{1,0:T(8,128)} fusion(bf16[1,1024,4096]{2,1,0:T(8,128)(2,1)} %all-gather.2.cloned.1.call-done, f32[2,4096]{1,0:T(2,128)S(1)} %gather_fusion.2, f32[2,4096]{1,0:T(2,128)S(1)} %gather_fusion.3, f32[2]{0:T(128)S(1)} %divide_subtract_fusion), kind=kOutput, calls=%fused_computation.12 | convolution fusion | flops 16801792 | bytes 8462344
  177.8 0.0 reduce-scatter.4.cloned.1.call-update
  177.8 20.4 %reduce-scatter.4.cloned.1.call-done = f32[256,2]{1,0:T(8,128)} async-done(((f32[1024,2]{1,0:T(8,128)}), f32[256,2]{1,0:T(8,128)}) %reduce-scatter.4.cloned.1.call-update) | async-done | bytes 2064
  198.2 1.6 copy.11
  (2 shorter events, 0.0 us)
Async XLA Ops:
  6.5 5.1 %copy-start = (bf16[1,128,5120]{2,1,0:T(8,128)(2,1)S(1)}, bf16[1,128,5120]{2,1,0:T(8,128)(2,1)}, u32[]{:S(2)}) copy-start(bf16[1,128,5120]{2,1,0:T(8,128)(2,1)} %param.7) | copy-start | bytes 3932164
  6.5 164.6 %all-gather.2.cloned.1.call-start = ((), (), s32[]{:S(2)}) async-start(), calls=%async_computation.1 | async-start | bytes 8454144 | tf_op jit(solution)/shard_map/all_gather | solution.py:28
  7.3 190.9 %reduce-scatter.4.cloned.1.call-start = ((), (), s32[]{:S(2)}) async-start(), calls=%async_computation.2 | async-start | bytes 655360
  11.6 2.0 copy-start.1
  11.6 2.1 %copy-start.2 = (bf16[1,5120,128]{2,1,0:T(8,128)(2,1)S(1)}, bf16[1,5120,128]{2,1,0:T(8,128)(2,1)}, u32[]{:S(2)}) copy-start(bf16[1,5120,128]{2,1,0:T(8,128)(2,1)} %param.9) | copy-start | bytes 3932164
Sparse Core Ops, SparseCore 0:
  11.7 159.3 all-gather.1
  177.9 20.2 reduce-scatter.3
where the time goes:
time: 207 us
  waiting for transfers between devices  176 us (85%)
  between operations  13.4 us (6%)
  matrix products  9.66 us (5%)
  local copies, waits for them, and re-layouts  5.54 us (3%)
    all_gather x1, waiting for transfers between devices, local(): lax.all_gather(queries, 'dp', axis=1, tiled=True)[0]  155 us
    unnamed x3, waiting for transfers between devices  21.1 us
    unnamed x1, matrix products  6.59 us
  transfers between devices with their start and end apart: 2, of which 2 were waited for; matrix products, arithmetic and copies ran while one was open for 4% of the time, Pallas kernels for 0%

commit v1 on v0

v1 whole, which is shorter than its diff:
```python
import jax
import jax.numpy as jnp
from jax import lax
from jax.experimental import pallas as pl
from jax.experimental.pallas import tpu as pltpu
from jax.sharding import Mesh, PartitionSpec as P

DP = ("zh", "zl", "x", "yhh", "yhl")
PAIR_AXES = ("zl", "x", "yhh")
QUERY_AXES = ("zh", "yhl")
CHUNKS = 4
F32 = jnp.float32
BF16 = jnp.bfloat16


def train_kernel(act, grad, proj, rewards, lengths, pairing, out, rows_v, proj_v, outer, sems):
    tokens, width = act.shape[1], act.shape[2]
    step = width // CHUNKS
    copies = []
    for i in range(CHUNKS):
        cols = pl.ds(i * step, step)
        copies.append([
            pltpu.make_async_copy(act.at[0, :, cols], rows_v.at[pl.ds(0, tokens), cols], sems.at[i, 0]),
            pltpu.make_async_copy(grad.at[0, :, cols], rows_v.at[pl.ds(tokens, tokens), cols], sems.at[i, 1]),
            pltpu.make_async_copy(proj.at[0, cols, :], proj_v.at[cols, :], sems.at[i, 2]),
        ])
        for c in copies[-1]:
            c.start()
    half = proj.shape[2] // 2
    seqs = lengths.shape[0]
    slots = tokens // seqs
    pairs = pairing.shape[0]
    place = lax.broadcasted_iota(jnp.int32, (slots, half), 0)
    signs, weights = [], []
    for p in range(pairs):
        chosen, rejected = pairing[p, 0], pairing[p, 1]
        blocks = []
        margin = jnp.float32(0)
        for s in range(seqs):
            coef = jnp.where(rejected == s, 1.0, 0.0) - jnp.where(chosen == s, 1.0, 0.0)
            blocks.append(jnp.where(place < lengths[s], coef, 0.0))
            margin = jnp.where(chosen == s, margin + rewards[s], margin)
        for s in range(seqs):
            margin = jnp.where(rejected == s, margin - rewards[s], margin)
        signs.append(jnp.concatenate(blocks, axis=0))
        weights.append(1.0 - jax.nn.sigmoid(jnp.full((half, half), margin, F32)))
    total = jnp.zeros((2 * tokens, 2 * half), F32)
    for i in range(CHUNKS):
        for c in copies[i]:
            c.wait()
        cols = pl.ds(i * step, step)
        total += jnp.dot(rows_v[:, cols], proj_v[cols, :], preferred_element_type=F32)
    a = total[:tokens, :half]
    g = total[tokens:, half:]
    g = jnp.concatenate([g * s for s in signs], axis=1)
    g_hi = g.astype(BF16)
    g_lo = (g - g_hi.astype(F32)).astype(BF16)
    a_hi = a.astype(BF16)
    a_lo = (a - a_hi.astype(F32)).astype(BF16)

    def over_tokens(l, r):
        return lax.dot_general(l, r, (((0,), (0,)), ((), ())), preferred_element_type=F32)

    t = over_tokens(g_hi, a_hi) + (over_tokens(g_hi, a_lo) + over_tokens(g_lo, a_hi))
    outer[:, :half] = t * jnp.concatenate(weights, axis=0)
    parts = [outer[pl.ds(k, pairs * 8, stride=8), :half] for k in range(8)]
    flat = jnp.concatenate(parts, axis=1).astype(BF16)
    for n in range(out.shape[0]):
        out[n] = flat


def score_kernel(train, queries, out, train_f):
    members = train.shape[0]
    group = lax.axis_index("x")
    span = queries.shape[0] // 4
    for name in PAIR_AXES[2:]:
        group = group * lax.axis_size(name) + lax.axis_index(name)
    for j in range(4):
        train_f[j] = train[:, :, 128 * j : 128 * j + 128].reshape(train_f.shape[1:]).astype(F32)
    total = None
    for s in range(8):
        rows = [train_f[j, pl.ds(s, members * 2, stride=8), :].astype(BF16) for j in range(4)]
        rows = jnp.concatenate(rows, axis=1)
        term = lax.dot_general(
            rows, queries[:, pl.ds(512 * s, 512)], (((1,), (1,)), ((), ())), preferred_element_type=F32
        )
        total = term if total is None else total + term
    if total.shape[1] < 128:
        total = jnp.concatenate([total, jnp.zeros((total.shape[0], 128 - total.shape[1]), F32)], axis=1)
    lane = lax.broadcasted_iota(jnp.int32, total.shape, 1)
    for layer in range(4):
        mine = jnp.where(lane // span == layer, total, 0.0)
        shift = lax.rem(group * span + (128 - layer * span), 128)
        out[layer] = pltpu.roll(mine, shift, 1)


def sum_kernel(got, out):
    terms = got[...]
    group = got.shape[0] // 8
    for half in range(2):
        total = None
        for layer in range(4):
            for k in range(group):
                term = terms[(layer * 2 + half) * group + k]
                total = term if total is None else total + term
        out[:, 128 * half : 128 * half + 128] = total


def local(activations, out_grads, projectors, rewards, lengths, pairing, queries):
    tokens, width = activations.shape[1:]
    members = lax.axis_size(PAIR_AXES)
    holders = lax.axis_size(QUERY_AXES)
    hbm = pl.BlockSpec(memory_space=pltpu.HBM)
    smem = pl.BlockSpec(memory_space=pltpu.SMEM)
    vmem = pl.BlockSpec(memory_space=pltpu.VMEM)

    sent_queries = jnp.broadcast_to(queries, (holders,) + queries.shape[1:])
    held = lax.all_to_all(sent_queries, QUERY_AXES, 0, 0).reshape(-1, queries.shape[2])

    sent = pl.pallas_call(
        train_kernel,
        out_shape=jax.ShapeDtypeStruct((members, 16, 512), BF16),
        in_specs=[hbm, hbm, hbm, smem, smem, smem],
        out_specs=vmem,
        scratch_shapes=[
            pltpu.VMEM((2 * tokens, width), BF16),
            pltpu.VMEM((width, projectors.shape[2]), BF16),
            pltpu.VMEM((projectors.shape[2], projectors.shape[2]), F32),
            pltpu.SemaphoreType.DMA((CHUNKS, 3)),
        ],
        compiler_params=pltpu.CompilerParams(vmem_limit_bytes=60 << 20),
        cost_estimate=pl.CostEstimate(flops=8 * 256 * 5120 * 128, bytes_accessed=32 << 20, transcendentals=0),
        name="train",
    )(activations, out_grads, projectors, rewards, lengths, pairing)
    gathered = lax.all_to_all(sent, PAIR_AXES, 0, 0)

    partial = pl.pallas_call(
        score_kernel,
        out_shape=jax.ShapeDtypeStruct((4, members * 2, 128), F32),
        in_specs=[vmem, vmem],
        out_specs=vmem,
        scratch_shapes=[pltpu.VMEM((4, members * 16, 128), F32)],
        compiler_params=pltpu.CompilerParams(vmem_limit_bytes=16 << 20),
        cost_estimate=pl.CostEstimate(flops=2 * 32 * 64 * 4096, bytes_accessed=1 << 20, transcendentals=0),
        name="score",
    )(gathered, held)
    got = lax.all_to_all(partial.reshape(4 * members, 2, 128), ("layer",) + PAIR_AXES, 0, 0)
    return pl.pallas_call(
        sum_kernel,
        out_shape=jax.ShapeDtypeStruct((2, 256), F32),
        in_specs=[vmem],
        out_specs=vmem,
        name="total",
    )(got)


def solution(mesh):
    fine = Mesh(mesh.devices.reshape(4, 4, 2, 4, 2, 2), ("layer",) + DP)
    return jax.shard_map(
        local,
        mesh=fine,
        in_specs=(
            P("layer", DP, None),
            P("layer", DP, None),
            P("layer", None, None),
            P(DP),
            P(DP),
            P(DP, None),
            P("layer", DP, None),
        ),
        out_specs=P(DP, "layer"),
        check_vma=False,
    )
```

time: 207 us -> 73.8 us (0.36)
  waiting for transfers between devices: 176 us -> 0 us
  blocking collectives: 0 us -> 66.9 us
  between operations: 13.4 us -> 0.02 us
  matrix products: 9.66 us -> 0 us
  Pallas kernels: 0 us -> 6.54 us
  local copies, waits for them, and re-layouts: 5.54 us -> 0.04 us
    all_gather x1 -> x0, waiting for transfers between devices: 155 us -> none  [local(): lax.all_gather(queries, 'dp', axis=1, tiled=True)[0]]
    all_to_all x0 -> x3, blocking collectives: none -> 66.9 us  [the longest x1 24.1 us: local(): lax.all_to_all(partial.reshape(4 * members, 2, 128), ('layer',) + PAIR_AX...]
    unnamed x3 -> x0, waiting for transfers between devices: 21.1 us -> none
    unnamed x1 -> x0, matrix products: 6.59 us -> none
    pallas_call x0 -> x3, Pallas kernels: none -> 6.54 us  [the longest x1 4.73 us: local(): pl.pallas_call(train_kernel, out_shape=jax.ShapeDtypeStruct((members, 16,...]
    gather x4 -> x0, local copies, waits for them, and re-layouts: 3.73 us -> none  [the longest x2 2.59 us: local(): margin_weight = 1.0 - jax.nn.sigmoid(rewards[chosen] - rewards[rejected])]
    dot_general x3 -> x0, matrix products: 3.07 us -> none  [the longest x1 1.95 us: local(): jnp.dot(activations[0], projectors[0, :, :half], preferred_element_type=j...]
  transfers between devices with their start and end apart: 2 -> 0, of which waited for: 2 -> 0; matrix products, arithmetic and copies ran while one was open for 4% -> 0% of each run, Pallas kernels for 0% -> 0%
where the time goes in v1:
time: 73.8 us; the launch traced here: 73.5 us
  blocking collectives  66.9 us (91%)
  Pallas kernels  6.54 us (9%)
    all_to_all x1, blocking collectives, local(): lax.all_to_all(partial.reshape(4 * members, 2, 128), ('layer',) + PAIR_AX...  24.1 us
    all_to_all x1, blocking collectives, local(): gathered = lax.all_to_all(sent, PAIR_AXES, 0, 0)  22.2 us
    all_to_all x1, blocking collectives, local(): lax.all_to_all(sent_queries, QUERY_AXES, 0, 0).reshape(-1, queries.shape[2])  20.6 us
    pallas_call x1, Pallas kernels, local(): pl.pallas_call(train_kernel, out_shape=jax.ShapeDtypeStruct((members, 16,...  4.73 us

profile of v1, /device:TPU:1, one launch (start us, length us, event | category | flops | bytes accessed | tf_op | source)
XLA Modules:
  0.0 73.5 jit_solution(10814056844089255440)
XLA Ops:
  0.0 0.0 copy-start
  0.0 4.7 %train.1 = bf16[16,16,512]{2,1,0:T(8,128)(2,1)} custom-call(bf16[1,128,5120]{2,1,0:T(8,128)(2,1)} %act.1, bf16[1,128,5120]{2,1,0:T(8,128)(2,1)} %grad.1, bf16[1,5120,128]{2,1,0:T(8,128)(2,1)} %proj.1, f32[4]{0:T(128)} %rewards.1, s32[4]{0:T(128)} %lengths.1, s32[2,2]{1,0:T(2,128)} %pairing.1), custom_call_target="tpu_custom_call" | custom-call | flops 1342177280 | bytes 33554432 | tf_op jit(solution)/shard_map/train/pallas_call | solution.py:120
  4.7 22.2 %all_to_all.15.train = bf16[16,16,512]{2,1,0:T(8,128)(2,1)S(1)} all-to-all(bf16[16,16,512]{2,1,0:T(8,128)(2,1)} %train.1), channel_id=1, replica_groups=mesh['layer'=4,'zh'=4,'zl'=2,'x'=4,'yhh'=2,'yhl'=2] {'zl','x','yhh'}, dimensions={0} | all-to-all | bytes 524288 | tf_op jit(solution)/shard_map/all_to_all | solution.py:135
  27.0 0.0 copy-done
  27.0 20.6 %all_to_all.16 = bf16[8,8,4096]{2,1,0:T(8,128)(2,1)S(1)} all-to-all(bf16[8,8,4096]{2,1,0:T(8,128)(2,1)S(1)} %broadcast_in_dim.8), channel_id=1, replica_groups=mesh['layer'=4,'zh'=4,'zl'=2,'x'=4,'yhh'=2,'yhl'=2] {'zh','yhl'}, dimensions={0} | all-to-all | bytes 1048576 | tf_op jit(solution)/shard_map/all_to_all | solution.py:118
  47.6 0.4 score.1
  48.0 24.1 %all_to_all.17.got = f32[64,2,128]{2,1,0:T(2,128)} all-to-all(f32[64,2,128]{2,1,0:T(2,128)S(1)} %bitcast.4), channel_id=1, replica_groups=mesh['layer'=4,'zh'=4,'zl'=2,'x'=4,'yhh'=2,'yhl'=2] {'layer','zl','x','y..., dimensions={0} | all-to-all | bytes 131072 | tf_op jit(solution)/shard_map/all_to_all | solution.py:147
  72.1 1.5 %total.1 = f32[2,256]{1,0:T(2,128)} custom-call(f32[64,2,128]{2,1,0:T(2,128)} %all_to_all.17.got), custom_call_target="tpu_custom_call" | custom-call | tf_op jit(solution)/shard_map/total/pallas_call | solution.py:148
  (1 shorter events, 0.0 us)
Async XLA Ops:
  0.0 27.0 %copy-start = (bf16[1,8,4096]{2,1,0:T(8,128)(2,1)S(1)}, bf16[1,8,4096]{2,1,0:T(8,128)(2,1)}, u32[]{:S(2)}) copy-start(bf16[1,8,4096]{2,1,0:T(8,128)(2,1)} %param.13) | copy-start | bytes 196612

commit v2 on v1

--- a/solution.py
+++ b/solution.py
@@ -5,9 +5,9 @@
 from jax.experimental.pallas import tpu as pltpu
 from jax.sharding import Mesh, PartitionSpec as P
 
-DP = ("zh", "zl", "x", "yhh", "yhl")
-PAIR_AXES = ("zl", "x", "yhh")
-QUERY_AXES = ("zh", "yhl")
+DP = ("zh", "zm", "zl", "x", "yh")
+PAIR_AXES = ("zl", "zm", "zh")
+QUERY_AXES = (("yh",), ("x",))
 CHUNKS = 4
 F32 = jnp.float32
 BF16 = jnp.bfloat16
@@ -65,18 +65,13 @@
     outer[:, :half] = t * jnp.concatenate(weights, axis=0)
     parts = [outer[pl.ds(k, pairs * 8, stride=8), :half] for k in range(8)]
     flat = jnp.concatenate(parts, axis=1).astype(BF16)
-    for n in range(out.shape[0]):
-        out[n] = flat
+    out[...] = flat
 
 
 def score_kernel(train, queries, out, train_f):
-    members = train.shape[0]
-    group = lax.axis_index("x")
-    span = queries.shape[0] // 4
-    for name in PAIR_AXES[2:]:
-        group = group * lax.axis_size(name) + lax.axis_index(name)
+    members = train.shape[0] // 16
     for j in range(4):
-        train_f[j] = train[:, :, 128 * j : 128 * j + 128].reshape(train_f.shape[1:]).astype(F32)
+        train_f[j] = train[:, 128 * j : 128 * j + 128].astype(F32)
     total = None
     for s in range(8):
         rows = [train_f[j, pl.ds(s, members * 2, stride=8), :].astype(BF16) for j in range(4)]
@@ -85,41 +80,29 @@
             rows, queries[:, pl.ds(512 * s, 512)], (((1,), (1,)), ((), ())), preferred_element_type=F32
         )
         total = term if total is None else total + term
-    if total.shape[1] < 128:
-        total = jnp.concatenate([total, jnp.zeros((total.shape[0], 128 - total.shape[1]), F32)], axis=1)
-    lane = lax.broadcasted_iota(jnp.int32, total.shape, 1)
+    mine = lax.axis_index("zh") * 2 + lax.axis_index("zm")
     for layer in range(4):
-        mine = jnp.where(lane // span == layer, total, 0.0)
-        shift = lax.rem(group * span + (128 - layer * span), 128)
-        out[layer] = pltpu.roll(mine, shift, 1)
+        out[layer] = jnp.where(mine == layer, total, 0.0)
 
 
 def sum_kernel(got, out):
-    terms = got[...]
-    group = got.shape[0] // 8
     for half in range(2):
-        total = None
-        for layer in range(4):
-            for k in range(group):
-                term = terms[(layer * 2 + half) * group + k]
-                total = term if total is None else total + term
+        total = got[0, half]
+        for k in range(1, got.shape[0]):
+            total = total + got[k, half]
         out[:, 128 * half : 128 * half + 128] = total
 
 
 def local(activations, out_grads, projectors, rewards, lengths, pairing, queries):
     tokens, width = activations.shape[1:]
     members = lax.axis_size(PAIR_AXES)
-    holders = lax.axis_size(QUERY_AXES)
     hbm = pl.BlockSpec(memory_space=pltpu.HBM)
     smem = pl.BlockSpec(memory_space=pltpu.SMEM)
     vmem = pl.BlockSpec(memory_space=pltpu.VMEM)
 
-    sent_queries = jnp.broadcast_to(queries, (holders,) + queries.shape[1:])
-    held = lax.all_to_all(sent_queries, QUERY_AXES, 0, 0).reshape(-1, queries.shape[2])
-
-    sent = pl.pallas_call(
+    train = pl.pallas_call(
         train_kernel,
-        out_shape=jax.ShapeDtypeStruct((members, 16, 512), BF16),
+        out_shape=jax.ShapeDtypeStruct((16, 512), BF16),
         in_specs=[hbm, hbm, hbm, smem, smem, smem],
         out_specs=vmem,
         scratch_shapes=[
@@ -128,11 +111,21 @@
             pltpu.VMEM((projectors.shape[2], projectors.shape[2]), F32),
             pltpu.SemaphoreType.DMA((CHUNKS, 3)),
         ],
-        compiler_params=pltpu.CompilerParams(vmem_limit_bytes=60 << 20),
-        cost_estimate=pl.CostEstimate(flops=8 * 256 * 5120 * 128, bytes_accessed=32 << 20, transcendentals=0),
+        compiler_params=pltpu.CompilerParams(vmem_limit_bytes=62200000),
+        cost_estimate=pl.CostEstimate(flops=2 * 256 * 5120 * 128, bytes_accessed=4 << 20, transcendentals=0),
         name="train",
     )(activations, out_grads, projectors, rewards, lengths, pairing)
-    gathered = lax.all_to_all(sent, PAIR_AXES, 0, 0)
+    held = queries[0]
+    gathers = list(PAIR_AXES)
+    for stage, axes in enumerate(QUERY_AXES):
+        copies = jnp.broadcast_to(held, (lax.axis_size(axes),) + held.shape)
+        held = lax.all_to_all(copies, axes, 0, 0).reshape(-1, held.shape[1])
+        if stage == 0:
+            for axis in gathers[:1]:
+                train = lax.all_gather(train, axis, axis=0, tiled=True)
+            held, train = lax.optimization_barrier((held, train))
+    for axis in gathers[1:]:
+        train = lax.all_gather(train, axis, axis=0, tiled=True)
 
     partial = pl.pallas_call(
         score_kernel,
@@ -143,19 +136,20 @@
         compiler_params=pltpu.CompilerParams(vmem_limit_bytes=16 << 20),
         cost_estimate=pl.CostEstimate(flops=2 * 32 * 64 * 4096, bytes_accessed=1 << 20, transcendentals=0),
         name="score",
-    )(gathered, held)
-    got = lax.all_to_all(partial.reshape(4 * members, 2, 128), ("layer",) + PAIR_AXES, 0, 0)
+    )(train, held)
+    got = lax.all_to_all(partial.reshape(4 * members, 2, 128), ("layer", "zh", "zm", "zl"), 0, 0)
     return pl.pallas_call(
         sum_kernel,
         out_shape=jax.ShapeDtypeStruct((2, 256), F32),
         in_specs=[vmem],
         out_specs=vmem,
+        compiler_params=pltpu.CompilerParams(vmem_limit_bytes=1 << 20),
         name="total",
-    )(got)
+    )(got.reshape(-1, 2, 2, 128))
 
 
 def solution(mesh):
-    fine = Mesh(mesh.devices.reshape(4, 4, 2, 4, 2, 2), ("layer",) + DP)
+    fine = Mesh(mesh.devices.reshape(4, 2, 2, 2, 4, 4), ("layer",) + DP)
     return jax.shard_map(
         local,
         mesh=fine,

time: 73.8 us -> 60.7 us (0.82)
  blocking collectives: 66.9 us -> 40.8 us
  starting transfers between devices: 0 us -> 11.5 us
  local copies, waits for them, and re-layouts: 0.04 us -> 2.62 us
  Pallas kernels: 6.54 us -> 5.45 us
    all_to_all x3 -> x1, blocking collectives: 66.9 us -> 21.2 us  [local(): lax.all_to_all(partial.reshape(4 * members, 2, 128), ('layer', 'zh', 'zm'...]
    all_gather x0 -> x3, blocking collectives: none -> 19.6 us  [local(): train = lax.all_gather(train, axis, axis=0, tiled=True)]
    all_to_all x0 -> x2, starting transfers between devices: none -> 11.5 us  [local(): held = lax.all_to_all(copies, axes, 0, 0).reshape(-1, held.shape[1])]
    broadcast_in_dim x1 -> x2, local copies, waits for them, and re-layouts: 0.03 us -> 2.62 us  [local(): copies = jnp.broadcast_to(held, (lax.axis_size(axes),) + held.shape)]
    pallas_call x1, Pallas kernels: 1.45 us -> 0.6 us  [local(): pl.pallas_call(sum_kernel, out_shape=jax.ShapeDtypeStruct((2, 256), F32),...]
  transfers between devices with their start and end apart: 0 -> 2, of which waited for: 0 -> 0; matrix products, arithmetic and copies ran while one was open for 0% -> 0% of each run, Pallas kernels for 0% -> 7%
where the time goes in v2:
time: 60.7 us; the launch traced here: 60.3 us
  blocking collectives  40.8 us (67%)
  starting transfers between devices  11.5 us (19%)
  Pallas kernels  5.45 us (9%)
  local copies, waits for them, and re-layouts  2.62 us (4%)
    all_to_all x1, blocking collectives, local(): lax.all_to_all(partial.reshape(4 * members, 2, 128), ('layer', 'zh', 'zm'...  21.2 us
    all_gather x3, blocking collectives, local(): train = lax.all_gather(train, axis, axis=0, tiled=True)  19.6 us
    all_to_all x2, starting transfers between devices, local(): held = lax.all_to_all(copies, axes, 0, 0).reshape(-1, held.shape[1])  11.5 us
    pallas_call x1, Pallas kernels, local(): pl.pallas_call(train_kernel, out_shape=jax.ShapeDtypeStruct((16, 512), BF...  4.48 us
    broadcast_in_dim x2, local copies, waits for them, and re-layouts, local(): copies = jnp.broadcast_to(held, (lax.axis_size(axes),) + held.shape)  2.62 us
  transfers between devices with their start and end apart: 2, of which 0 were waited for; matrix products, arithmetic and copies ran while one was open for 0% of the time, Pallas kernels for 7%

profile of v2, /device:TPU:1, one launch (start us, length us, event | category | flops | bytes accessed | tf_op | source)
XLA Modules:
  0.0 60.3 jit_solution(6862542332117357710)
XLA Ops:
  0.0 1.5 %broadcast_in_dim.6 = bf16[4,8,4096]{2,1,0:T(8,128)(2,1)} broadcast(bf16[8,4096]{1,0:T(8,128)(2,1)} %bitcast.9), dimensions={1,2} | broadcast | bytes 327680 | tf_op jit(solution)/shard_map/broadcast_in_dim | solution.py:121
  1.5 7.6 %all-to-all-start = ((bf16[4,8,4096]{2,1,0:T(8,128)(2,1)}), bf16[4,8,4096]{2,1,0:T(8,128)(2,1)S(1)}, u32[]{:S(2)}, u32[]{:S(2)}) async-start(bf16[4,8,4096]{2,1,0:T(8,128)(2,1)} %broadcast_in_dim.6), calls=%async_computation | async-start | bytes 524288 | tf_op jit(solution)/shard_map/all_to_all | solution.py:122
  9.2 4.5 %train.1 = bf16[16,512]{1,0:T(8,128)(2,1)} custom-call(bf16[1,128,5120]{2,1,0:T(8,128)(2,1)} %act.1, bf16[1,128,5120]{2,1,0:T(8,128)(2,1)} %grad.1, bf16[1,5120,128]{2,1,0:T(8,128)(2,1)} %proj.1, f32[4]{0:T(128)} %rewards.1, s32[4]{0:T(128)} %lengths.1, s32[2,2]{1,0:T(2,128)} %pairing.1), custom_call_target="tpu_custom_call" | custom-call | flops 335544320 | bytes 4194304 | tf_op jit(solution)/shard_map/train/pallas_call | solution.py:103
  13.7 4.4 %all_gather.9 = bf16[32,512]{1,0:T(8,128)(2,1)S(1)} all-gather(bf16[16,512]{1,0:T(8,128)(2,1)} %train.1), channel_id=1, replica_groups=mesh['layer'=4,'zh'=2,'zm'=2,'zl'=2,'x'=4,'yh'=4] {'zl'}, dimensions={0}, use_global_device_ids=true | all-gather | bytes 49152 | tf_op jit(solution)/shard_map/all_gather | solution.py:125
  18.1 0.0 all-to-all-done
  18.1 1.1 %broadcast_in_dim.7 = bf16[4,32,4096]{2,1,0:T(8,128)(2,1)} broadcast(bf16[32,4096]{1,0:T(8,128)(2,1)S(1)} %bitcast.8), dimensions={1,2} | broadcast | bytes 1310720 | tf_op jit(solution)/shard_map/broadcast_in_dim | solution.py:121
  19.2 3.8 %all-to-all-start.1 = ((bf16[4,32,4096]{2,1,0:T(8,128)(2,1)}), bf16[4,32,4096]{2,1,0:T(8,128)(2,1)S(1)}, u32[]{:S(2)}, u32[]{:S(2)}) async-start(bf16[4,32,4096]{2,1,0:T(8,128)(2,1)} %broadcast_in_dim.7), calls=%async_computation.1 | async-start | bytes 2097152 | tf_op jit(solution)/shard_map/all_to_all | solution.py:122
  23.0 5.8 %all_gather.10 = bf16[64,512]{1,0:T(8,128)(2,1)S(1)} all-gather(bf16[32,512]{1,0:T(8,128)(2,1)S(1)} %all_gather.9), channel_id=1, replica_groups=mesh['layer'=4,'zh'=2,'zm'=2,'zl'=2,'x'=4,'yh'=4] {'zm'}, dimensions={0}, use_global_device_ids=true | all-gather | bytes 98304 | tf_op jit(solution)/shard_map/all_gather | solution.py:128
  28.9 9.3 %all_gather.11.train = bf16[128,512]{1,0:T(8,128)(2,1)S(1)} all-gather(bf16[64,512]{1,0:T(8,128)(2,1)S(1)} %all_gather.10), channel_id=1, replica_groups=mesh['layer'=4,'zh'=2,'zm'=2,'zl'=2,'x'=4,'yh'=4] {'zh'}, dimensions={0}, use_global_device_ids=true | all-gather | bytes 196608 | tf_op jit(solution)/shard_map/all_gather | solution.py:128
  38.2 0.0 all-to-all-done.1
  38.2 0.4 score.1
  38.6 21.2 %all_to_all.15 = f32[32,2,128]{2,1,0:T(2,128)S(1)} all-to-all(f32[32,2,128]{2,1,0:T(2,128)S(1)} %bitcast.6), channel_id=1, replica_groups=mesh['layer'=4,'zh'=2,'zm'=2,'zl'=2,'x'=4,'yh'=4] {'layer','zh','zm','zl'}, dimensions={0} | all-to-all | bytes 65536 | tf_op jit(solution)/shard_map/all_to_all | solution.py:140
  59.7 0.6 total.1
Async XLA Ops:
  1.5 16.6 %all-to-all-start = ((bf16[4,8,4096]{2,1,0:T(8,128)(2,1)}), bf16[4,8,4096]{2,1,0:T(8,128)(2,1)S(1)}, u32[]{:S(2)}, u32[]{:S(2)}) async-start(bf16[4,8,4096]{2,1,0:T(8,128)(2,1)} %broadcast_in_dim.6), calls=%async_computation | async-start | bytes 524288 | tf_op jit(solution)/shard_map/all_to_all | solution.py:122
  19.2 19.0 %all-to-all-start.1 = ((bf16[4,32,4096]{2,1,0:T(8,128)(2,1)}), bf16[4,32,4096]{2,1,0:T(8,128)(2,1)S(1)}, u32[]{:S(2)}, u32[]{:S(2)}) async-start(bf16[4,32,4096]{2,1,0:T(8,128)(2,1)} %broadcast_in_dim.7), calls=%async_computation.1 | async-start | bytes 2097152 | tf_op jit(solution)/shard_map/all_to_all | solution.py:122

commit v3 on v2

--- a/solution.py
+++ b/solution.py
@@ -13,7 +13,13 @@
 BF16 = jnp.bfloat16
 
 
-def train_kernel(act, grad, proj, rewards, lengths, pairing, out, rows_v, proj_v, outer, sems):
+def train_kernel(
+    act, grad, proj, rewards_in, lengths_in, pairing_in, out, rows_v, proj_v, outer, rewards, lengths, pairing, sems, small
+):
+    given = [(rewards_in, rewards), (lengths_in, lengths), (pairing_in, pairing)]
+    scalars = [pltpu.make_async_copy(a, b, small.at[i]) for i, (a, b) in enumerate(given)]
+    for c in scalars:
+        c.start()
     tokens, width = act.shape[1], act.shape[2]
     step = width // CHUNKS
     copies = []
@@ -26,6 +32,8 @@
         ])
         for c in copies[-1]:
             c.start()
+    for c in scalars:
+        c.wait()
     half = proj.shape[2] // 2
     seqs = lengths.shape[0]
     slots = tokens // seqs
@@ -97,19 +105,22 @@
     tokens, width = activations.shape[1:]
     members = lax.axis_size(PAIR_AXES)
     hbm = pl.BlockSpec(memory_space=pltpu.HBM)
-    smem = pl.BlockSpec(memory_space=pltpu.SMEM)
     vmem = pl.BlockSpec(memory_space=pltpu.VMEM)
 
     train = pl.pallas_call(
         train_kernel,
         out_shape=jax.ShapeDtypeStruct((16, 512), BF16),
-        in_specs=[hbm, hbm, hbm, smem, smem, smem],
+        in_specs=[hbm] * 6,
         out_specs=vmem,
         scratch_shapes=[
             pltpu.VMEM((2 * tokens, width), BF16),
             pltpu.VMEM((width, projectors.shape[2]), BF16),
             pltpu.VMEM((projectors.shape[2], projectors.shape[2]), F32),
+            pltpu.SMEM(rewards.shape, rewards.dtype),
+            pltpu.SMEM(lengths.shape, lengths.dtype),
+            pltpu.SMEM(pairing.shape, pairing.dtype),
             pltpu.SemaphoreType.DMA((CHUNKS, 3)),
+            pltpu.SemaphoreType.DMA((3,)),
         ],
         compiler_params=pltpu.CompilerParams(vmem_limit_bytes=62200000),
         cost_estimate=pl.CostEstimate(flops=2 * 256 * 5120 * 128, bytes_accessed=4 << 20, transcendentals=0),

time: 60.7 us -> 60.7 us (level)
  Pallas kernels: 5.45 us -> 4.77 us
    pallas_call x1, Pallas kernels: 4.48 us -> 3.8 us  [local(): pl.pallas_call(train_kernel, out_shape=jax.ShapeDtypeStruct((16, 512), BF...]
  transfers between devices with their start and end apart: 2 -> 2, of which waited for: 0 -> 1; matrix products, arithmetic and copies ran while one was open for 0% -> 0% of each run, Pallas kernels for 7% -> 6%
where the time goes in v3:
time: 60.7 us; the launch traced here: 60.3 us
  blocking collectives  41.3 us (68%)
  starting transfers between devices  11.2 us (18%)
  Pallas kernels  4.77 us (8%)
  local copies, waits for them, and re-layouts  2.62 us (4%)
    all_to_all x1, blocking collectives, local(): lax.all_to_all(partial.reshape(4 * members, 2, 128), ('layer', 'zh', 'zm'...  21.3 us
    all_gather x3, blocking collectives, local(): train = lax.all_gather(train, axis, axis=0, tiled=True)  20 us
    all_to_all x2, starting transfers between devices, local(): held = lax.all_to_all(copies, axes, 0, 0).reshape(-1, held.shape[1])  11.2 us
    pallas_call x1, Pallas kernels, local(): pl.pallas_call(train_kernel, out_shape=jax.ShapeDtypeStruct((16, 512), BF...  3.8 us
    broadcast_in_dim x2, local copies, waits for them, and re-layouts, local(): copies = jnp.broadcast_to(held, (lax.axis_size(axes),) + held.shape)  2.62 us
  transfers between devices with their start and end apart: 2, of which 1 were waited for; matrix products, arithmetic and copies ran while one was open for 0% of the time, Pallas kernels for 6%

profile of v3, /device:TPU:1, one launch (start us, length us, event | category | flops | bytes accessed | tf_op | source)
XLA Modules:
  0.0 60.3 jit_solution(2619088868904891954)
XLA Ops:
  0.0 1.5 %broadcast_in_dim.6 = bf16[4,8,4096]{2,1,0:T(8,128)(2,1)} broadcast(bf16[8,4096]{1,0:T(8,128)(2,1)} %bitcast.9), dimensions={1,2} | broadcast | bytes 327680 | tf_op jit(solution)/shard_map/broadcast_in_dim | solution.py:132
  1.5 7.6 %all-to-all-start = ((bf16[4,8,4096]{2,1,0:T(8,128)(2,1)}), bf16[4,8,4096]{2,1,0:T(8,128)(2,1)S(1)}, u32[]{:S(2)}, u32[]{:S(2)}) async-start(bf16[4,8,4096]{2,1,0:T(8,128)(2,1)} %broadcast_in_dim.6), calls=%async_computation | async-start | bytes 524288 | tf_op jit(solution)/shard_map/all_to_all | solution.py:133
  9.2 3.8 %train.1 = bf16[16,512]{1,0:T(8,128)(2,1)} custom-call(bf16[1,128,5120]{2,1,0:T(8,128)(2,1)} %act.1, bf16[1,128,5120]{2,1,0:T(8,128)(2,1)} %grad.1, bf16[1,5120,128]{2,1,0:T(8,128)(2,1)} %proj.1, f32[4]{0:T(128)} %rewards_in.1, s32[4]{0:T(128)} %lengths_in.1, s32[2,2]{1,0:T(2,128)} %pairing_in.1), custom_call_target="tpu_custom_call" | custom-call | flops 335544320 | bytes 4194304 | tf_op jit(solution)/shard_map/train/pallas_call | solution.py:110
  13.0 4.5 %all_gather.9 = bf16[32,512]{1,0:T(8,128)(2,1)S(1)} all-gather(bf16[16,512]{1,0:T(8,128)(2,1)} %train.1), channel_id=1, replica_groups=mesh['layer'=4,'zh'=2,'zm'=2,'zl'=2,'x'=4,'yh'=4] {'zl'}, dimensions={0}, use_global_device_ids=true | all-gather | bytes 49152 | tf_op jit(solution)/shard_map/all_gather | solution.py:136
  17.5 0.5 all-to-all-done
  17.9 1.1 %broadcast_in_dim.7 = bf16[4,32,4096]{2,1,0:T(8,128)(2,1)} broadcast(bf16[32,4096]{1,0:T(8,128)(2,1)S(1)} %bitcast.8), dimensions={1,2} | broadcast | bytes 1310720 | tf_op jit(solution)/shard_map/broadcast_in_dim | solution.py:132
  19.0 3.6 %all-to-all-start.1 = ((bf16[4,32,4096]{2,1,0:T(8,128)(2,1)}), bf16[4,32,4096]{2,1,0:T(8,128)(2,1)S(1)}, u32[]{:S(2)}, u32[]{:S(2)}) async-start(bf16[4,32,4096]{2,1,0:T(8,128)(2,1)} %broadcast_in_dim.7), calls=%async_computation.1 | async-start | bytes 2097152 | tf_op jit(solution)/shard_map/all_to_all | solution.py:133
  22.5 5.8 %all_gather.10 = bf16[64,512]{1,0:T(8,128)(2,1)S(1)} all-gather(bf16[32,512]{1,0:T(8,128)(2,1)S(1)} %all_gather.9), channel_id=1, replica_groups=mesh['layer'=4,'zh'=2,'zm'=2,'zl'=2,'x'=4,'yh'=4] {'zm'}, dimensions={0}, use_global_device_ids=true | all-gather | bytes 98304 | tf_op jit(solution)/shard_map/all_gather | solution.py:139
  28.4 9.7 %all_gather.11.train = bf16[128,512]{1,0:T(8,128)(2,1)S(1)} all-gather(bf16[64,512]{1,0:T(8,128)(2,1)S(1)} %all_gather.10), channel_id=1, replica_groups=mesh['layer'=4,'zh'=2,'zm'=2,'zl'=2,'x'=4,'yh'=4] {'zh'}, dimensions={0}, use_global_device_ids=true | all-gather | bytes 196608 | tf_op jit(solution)/shard_map/all_gather | solution.py:139
  38.0 0.0 all-to-all-done.1
  38.1 0.4 score.1
  38.4 21.3 %all_to_all.15 = f32[32,2,128]{2,1,0:T(2,128)S(1)} all-to-all(f32[32,2,128]{2,1,0:T(2,128)S(1)} %bitcast.6), channel_id=1, replica_groups=mesh['layer'=4,'zh'=2,'zm'=2,'zl'=2,'x'=4,'yh'=4] {'layer','zh','zm','zl'}, dimensions={0} | all-to-all | bytes 65536 | tf_op jit(solution)/shard_map/all_to_all | solution.py:151
  59.7 0.6 total.1
Async XLA Ops:
  1.5 16.4 %all-to-all-start = ((bf16[4,8,4096]{2,1,0:T(8,128)(2,1)}), bf16[4,8,4096]{2,1,0:T(8,128)(2,1)S(1)}, u32[]{:S(2)}, u32[]{:S(2)}) async-start(bf16[4,8,4096]{2,1,0:T(8,128)(2,1)} %broadcast_in_dim.6), calls=%async_computation | async-start | bytes 524288 | tf_op jit(solution)/shard_map/all_to_all | solution.py:133
  19.0 19.1 %all-to-all-start.1 = ((bf16[4,32,4096]{2,1,0:T(8,128)(2,1)}), bf16[4,32,4096]{2,1,0:T(8,128)(2,1)S(1)}, u32[]{:S(2)}, u32[]{:S(2)}) async-start(bf16[4,32,4096]{2,1,0:T(8,128)(2,1)} %broadcast_in_dim.7), calls=%async_computation.1 | async-start | bytes 2097152 | tf_op jit(solution)/shard_map/all_to_all | solution.py:133

commit v4 on v3

--- a/solution.py
+++ b/solution.py
@@ -6,7 +6,7 @@
 from jax.sharding import Mesh, PartitionSpec as P
 
 DP = ("zh", "zm", "zl", "x", "yh")
-PAIR_AXES = ("zl", "zm", "zh")
+PAIR_AXES = ("zm", "zl", "zh")
 QUERY_AXES = (("yh",), ("x",))
 CHUNKS = 4
 F32 = jnp.float32
@@ -95,9 +95,10 @@
 
 def sum_kernel(got, out):
     for half in range(2):
-        total = got[0, half]
-        for k in range(1, got.shape[0]):
-            total = total + got[k, half]
+        total = None
+        for k in range(got.shape[0]):
+            for n in range(got.shape[2]):
+                total = got[k, half, n] if total is None else total + got[k, half, n]
         out[:, 128 * half : 128 * half + 128] = total
 
 
@@ -148,7 +149,7 @@
         cost_estimate=pl.CostEstimate(flops=2 * 32 * 64 * 4096, bytes_accessed=1 << 20, transcendentals=0),
         name="score",
     )(train, held)
-    got = lax.all_to_all(partial.reshape(4 * members, 2, 128), ("layer", "zh", "zm", "zl"), 0, 0)
+    got = lax.all_to_all(partial.reshape(4 * members, 2, 128), ("layer",) + PAIR_AXES[::-1], 0, 0)
     return pl.pallas_call(
         sum_kernel,
         out_shape=jax.ShapeDtypeStruct((2, 256), F32),
@@ -156,7 +157,7 @@
         out_specs=vmem,
         compiler_params=pltpu.CompilerParams(vmem_limit_bytes=1 << 20),
         name="total",
-    )(got.reshape(-1, 2, 2, 128))
+    )(got.reshape(-1, 2, 2, 2, 128))
 
 
 def solution(mesh):

time: 60.7 us -> 60 us (0.988)
  blocking collectives: 41.3 us -> 40 us
  starting transfers between devices: 11.2 us -> 11.9 us
    all_gather x3, blocking collectives: 20 us -> 18.9 us  [local(): train = lax.all_gather(train, axis, axis=0, tiled=True)]
    all_to_all x2, starting transfers between devices: 11.2 us -> 11.9 us  [local(): held = lax.all_to_all(copies, axes, 0, 0).reshape(-1, held.shape[1])]
where the time goes in v4:
time: 60 us; the launch traced here: 59.7 us
  blocking collectives  40 us (67%)
  starting transfers between devices  11.9 us (20%)
  Pallas kernels  4.77 us (8%)
  local copies, waits for them, and re-layouts  2.62 us (4%)
    all_to_all x1, blocking collectives, local(): lax.all_to_all(partial.reshape(4 * members, 2, 128), ('layer',) + PAIR_AX...  21 us
    all_gather x3, blocking collectives, local(): train = lax.all_gather(train, axis, axis=0, tiled=True)  18.9 us
    all_to_all x2, starting transfers between devices, local(): held = lax.all_to_all(copies, axes, 0, 0).reshape(-1, held.shape[1])  11.9 us
    pallas_call x1, Pallas kernels, local(): pl.pallas_call(train_kernel, out_shape=jax.ShapeDtypeStruct((16, 512), BF...  3.8 us
    broadcast_in_dim x2, local copies, waits for them, and re-layouts, local(): copies = jnp.broadcast_to(held, (lax.axis_size(axes),) + held.shape)  2.62 us
  transfers between devices with their start and end apart: 2, of which 1 were waited for; matrix products, arithmetic and copies ran while one was open for 0% of the time, Pallas kernels for 6%

profile of v4, /device:TPU:1, one launch (start us, length us, event | category | flops | bytes accessed | tf_op | source)
XLA Modules:
  0.0 59.7 jit_solution(15528013635384653993)
XLA Ops:
  0.0 1.5 %broadcast_in_dim.6 = bf16[4,8,4096]{2,1,0:T(8,128)(2,1)} broadcast(bf16[8,4096]{1,0:T(8,128)(2,1)} %bitcast.9), dimensions={1,2} | broadcast | bytes 327680 | tf_op jit(solution)/shard_map/broadcast_in_dim | solution.py:133
  1.5 7.6 %all-to-all-start = ((bf16[4,8,4096]{2,1,0:T(8,128)(2,1)}), bf16[4,8,4096]{2,1,0:T(8,128)(2,1)S(1)}, u32[]{:S(2)}, u32[]{:S(2)}) async-start(bf16[4,8,4096]{2,1,0:T(8,128)(2,1)} %broadcast_in_dim.6), calls=%async_computation | async-start | bytes 524288 | tf_op jit(solution)/shard_map/all_to_all | solution.py:134
  9.2 3.8 %train.1 = bf16[16,512]{1,0:T(8,128)(2,1)} custom-call(bf16[1,128,5120]{2,1,0:T(8,128)(2,1)} %act.1, bf16[1,128,5120]{2,1,0:T(8,128)(2,1)} %grad.1, bf16[1,5120,128]{2,1,0:T(8,128)(2,1)} %proj.1, f32[4]{0:T(128)} %rewards_in.1, s32[4]{0:T(128)} %lengths_in.1, s32[2,2]{1,0:T(2,128)} %pairing_in.1), custom_call_target="tpu_custom_call" | custom-call | flops 335544320 | bytes 4194304 | tf_op jit(solution)/shard_map/train/pallas_call | solution.py:111
  13.0 6.0 %all_gather.9 = bf16[32,512]{1,0:T(8,128)(2,1)S(1)} all-gather(bf16[16,512]{1,0:T(8,128)(2,1)} %train.1), channel_id=1, replica_groups=mesh['layer'=4,'zh'=2,'zm'=2,'zl'=2,'x'=4,'yh'=4] {'zm'}, dimensions={0}, use_global_device_ids=true | all-gather | bytes 49152 | tf_op jit(solution)/shard_map/all_gather | solution.py:137
  19.0 0.0 all-to-all-done
  19.0 1.1 %broadcast_in_dim.7 = bf16[4,32,4096]{2,1,0:T(8,128)(2,1)} broadcast(bf16[32,4096]{1,0:T(8,128)(2,1)S(1)} %bitcast.8), dimensions={1,2} | broadcast | bytes 1310720 | tf_op jit(solution)/shard_map/broadcast_in_dim | solution.py:133
  20.1 4.3 %all-to-all-start.1 = ((bf16[4,32,4096]{2,1,0:T(8,128)(2,1)}), bf16[4,32,4096]{2,1,0:T(8,128)(2,1)S(1)}, u32[]{:S(2)}, u32[]{:S(2)}) async-start(bf16[4,32,4096]{2,1,0:T(8,128)(2,1)} %broadcast_in_dim.7), calls=%async_computation.1 | async-start | bytes 2097152 | tf_op jit(solution)/shard_map/all_to_all | solution.py:134
  24.4 4.0 %all_gather.10 = bf16[64,512]{1,0:T(8,128)(2,1)S(1)} all-gather(bf16[32,512]{1,0:T(8,128)(2,1)S(1)} %all_gather.9), channel_id=1, replica_groups=mesh['layer'=4,'zh'=2,'zm'=2,'zl'=2,'x'=4,'yh'=4] {'zl'}, dimensions={0}, use_global_device_ids=true | all-gather | bytes 98304 | tf_op jit(solution)/shard_map/all_gather | solution.py:140
  28.4 8.9 %all_gather.11.train = bf16[128,512]{1,0:T(8,128)(2,1)S(1)} all-gather(bf16[64,512]{1,0:T(8,128)(2,1)S(1)} %all_gather.10), channel_id=1, replica_groups=mesh['layer'=4,'zh'=2,'zm'=2,'zl'=2,'x'=4,'yh'=4] {'zh'}, dimensions={0}, use_global_device_ids=true | all-gather | bytes 196608 | tf_op jit(solution)/shard_map/all_gather | solution.py:140
  37.3 0.4 all-to-all-done.1
  37.7 0.4 score.1
  38.0 21.0 %all_to_all.15 = f32[32,2,128]{2,1,0:T(2,128)S(1)} all-to-all(f32[32,2,128]{2,1,0:T(2,128)S(1)} %bitcast.6), channel_id=1, replica_groups=mesh['layer'=4,'zh'=2,'zm'=2,'zl'=2,'x'=4,'yh'=4] {'layer','zh','zl','zm'}, dimensions={0} | all-to-all | bytes 65536 | tf_op jit(solution)/shard_map/all_to_all | solution.py:152
  59.1 0.6 total.1
Async XLA Ops:
  1.5 17.4 %all-to-all-start = ((bf16[4,8,4096]{2,1,0:T(8,128)(2,1)}), bf16[4,8,4096]{2,1,0:T(8,128)(2,1)S(1)}, u32[]{:S(2)}, u32[]{:S(2)}) async-start(bf16[4,8,4096]{2,1,0:T(8,128)(2,1)} %broadcast_in_dim.6), calls=%async_computation | async-start | bytes 524288 | tf_op jit(solution)/shard_map/all_to_all | solution.py:134
  20.1 17.6 %all-to-all-start.1 = ((bf16[4,32,4096]{2,1,0:T(8,128)(2,1)}), bf16[4,32,4096]{2,1,0:T(8,128)(2,1)S(1)}, u32[]{:S(2)}, u32[]{:S(2)}) async-start(bf16[4,32,4096]{2,1,0:T(8,128)(2,1)} %broadcast_in_dim.7), calls=%async_computation.1 | async-start | bytes 2097152 | tf_op jit(solution)/shard_map/all_to_all | solution.py:134

commit v5 on v4

--- a/solution.py
+++ b/solution.py
@@ -110,7 +110,7 @@
 
     train = pl.pallas_call(
         train_kernel,
-        out_shape=jax.ShapeDtypeStruct((16, 512), BF16),
+        out_shape=pltpu.VMEM((16, 512), BF16),
         in_specs=[hbm] * 6,
         out_specs=vmem,
         scratch_shapes=[

time: 60 us -> 59.8 us (level)
  blocking collectives: 40 us -> 41.3 us
    all_gather x3, blocking collectives: 18.9 us -> 19.7 us  [local(): train = lax.all_gather(train, axis, axis=0, tiled=True)]
  transfers between devices with their start and end apart: 2 -> 2, of which waited for: 1 -> 0; matrix products, arithmetic and copies ran while one was open for 0% -> 0% of each run, Pallas kernels for 6% -> 5%
where the time goes in v5:
time: 59.8 us; the launch traced here: 59.4 us
  blocking collectives  41.3 us (69%)
  starting transfers between devices  11.4 us (19%)
  Pallas kernels  4.17 us (7%)
  local copies, waits for them, and re-layouts  2.62 us (4%)
    all_to_all x1, blocking collectives, local(): lax.all_to_all(partial.reshape(4 * members, 2, 128), ('layer',) + PAIR_AX...  21.5 us
    all_gather x3, blocking collectives, local(): train = lax.all_gather(train, axis, axis=0, tiled=True)  19.7 us
    all_to_all x2, starting transfers between devices, local(): held = lax.all_to_all(copies, axes, 0, 0).reshape(-1, held.shape[1])  11.4 us
    pallas_call x1, Pallas kernels, local(): pl.pallas_call(train_kernel, out_shape=pltpu.VMEM((16, 512), BF16), in_sp...  3.2 us
    broadcast_in_dim x2, local copies, waits for them, and re-layouts, local(): copies = jnp.broadcast_to(held, (lax.axis_size(axes),) + held.shape)  2.62 us
  transfers between devices with their start and end apart: 2, of which 0 were waited for; matrix products, arithmetic and copies ran while one was open for 0% of the time, Pallas kernels for 5%

profile of v5, /device:TPU:1, one launch (start us, length us, event | category | flops | bytes accessed | tf_op | source)
XLA Modules:
  0.0 59.4 jit_solution(10191141472157346522)
XLA Ops:
  0.0 1.5 %broadcast_in_dim.6 = bf16[4,8,4096]{2,1,0:T(8,128)(2,1)} broadcast(bf16[8,4096]{1,0:T(8,128)(2,1)} %bitcast.9), dimensions={1,2} | broadcast | bytes 327680 | tf_op jit(solution)/shard_map/broadcast_in_dim | solution.py:133
  1.5 7.6 %all-to-all-start = ((bf16[4,8,4096]{2,1,0:T(8,128)(2,1)}), bf16[4,8,4096]{2,1,0:T(8,128)(2,1)S(1)}, u32[]{:S(2)}, u32[]{:S(2)}) async-start(bf16[4,8,4096]{2,1,0:T(8,128)(2,1)} %broadcast_in_dim.6), calls=%async_computation | async-start | bytes 524288 | tf_op jit(solution)/shard_map/all_to_all | solution.py:134
  9.2 3.2 %train.1 = bf16[16,512]{1,0:T(8,128)(2,1)S(1)} custom-call(bf16[1,128,5120]{2,1,0:T(8,128)(2,1)} %act.1, bf16[1,128,5120]{2,1,0:T(8,128)(2,1)} %grad.1, bf16[1,5120,128]{2,1,0:T(8,128)(2,1)} %proj.1, f32[4]{0:T(128)} %rewards_in.1, s32[4]{0:T(128)} %lengths_in.1, s32[2,2]{1,0:T(2,128)} %pairing_in.1), custom_call_target="tpu_custom_call" | custom-call | flops 335544320 | bytes 4194304 | tf_op jit(solution)/shard_map/train/pallas_call | solution.py:111
  12.4 6.0 %all_gather.9 = bf16[32,512]{1,0:T(8,128)(2,1)S(1)} all-gather(bf16[16,512]{1,0:T(8,128)(2,1)S(1)} %train.1), channel_id=1, replica_groups=mesh['layer'=4,'zh'=2,'zm'=2,'zl'=2,'x'=4,'yh'=4] {'zm'}, dimensions={0}, use_global_device_ids=true | all-gather | bytes 49152 | tf_op jit(solution)/shard_map/all_gather | solution.py:137
  18.4 0.0 all-to-all-done
  18.4 1.1 %broadcast_in_dim.7 = bf16[4,32,4096]{2,1,0:T(8,128)(2,1)} broadcast(bf16[32,4096]{1,0:T(8,128)(2,1)S(1)} %bitcast.8), dimensions={1,2} | broadcast | bytes 1310720 | tf_op jit(solution)/shard_map/broadcast_in_dim | solution.py:133
  19.5 3.7 %all-to-all-start.1 = ((bf16[4,32,4096]{2,1,0:T(8,128)(2,1)}), bf16[4,32,4096]{2,1,0:T(8,128)(2,1)S(1)}, u32[]{:S(2)}, u32[]{:S(2)}) async-start(bf16[4,32,4096]{2,1,0:T(8,128)(2,1)} %broadcast_in_dim.7), calls=%async_computation.1 | async-start | bytes 2097152 | tf_op jit(solution)/shard_map/all_to_all | solution.py:134
  23.2 4.0 %all_gather.10 = bf16[64,512]{1,0:T(8,128)(2,1)S(1)} all-gather(bf16[32,512]{1,0:T(8,128)(2,1)S(1)} %all_gather.9), channel_id=1, replica_groups=mesh['layer'=4,'zh'=2,'zm'=2,'zl'=2,'x'=4,'yh'=4] {'zl'}, dimensions={0}, use_global_device_ids=true | all-gather | bytes 98304 | tf_op jit(solution)/shard_map/all_gather | solution.py:140
  27.2 9.7 %all_gather.11.train = bf16[128,512]{1,0:T(8,128)(2,1)S(1)} all-gather(bf16[64,512]{1,0:T(8,128)(2,1)S(1)} %all_gather.10), channel_id=1, replica_groups=mesh['layer'=4,'zh'=2,'zm'=2,'zl'=2,'x'=4,'yh'=4] {'zh'}, dimensions={0}, use_global_device_ids=true | all-gather | bytes 196608 | tf_op jit(solution)/shard_map/all_gather | solution.py:140
  36.9 0.0 all-to-all-done.1
  36.9 0.4 score.1
  37.3 21.5 %all_to_all.15 = f32[32,2,128]{2,1,0:T(2,128)S(1)} all-to-all(f32[32,2,128]{2,1,0:T(2,128)S(1)} %bitcast.6), channel_id=1, replica_groups=mesh['layer'=4,'zh'=2,'zm'=2,'zl'=2,'x'=4,'yh'=4] {'layer','zh','zl','zm'}, dimensions={0} | all-to-all | bytes 65536 | tf_op jit(solution)/shard_map/all_to_all | solution.py:152
  58.8 0.6 %total.1 = f32[2,256]{1,0:T(2,128)} custom-call(f32[8,2,2,2,128]{4,3,2,1,0:T(2,128)S(1)} %bitcast.7), custom_call_target="tpu_custom_call" | custom-call | tf_op jit(solution)/shard_map/total/pallas_call | solution.py:153
Async XLA Ops:
  1.5 16.8 %all-to-all-start = ((bf16[4,8,4096]{2,1,0:T(8,128)(2,1)}), bf16[4,8,4096]{2,1,0:T(8,128)(2,1)S(1)}, u32[]{:S(2)}, u32[]{:S(2)}) async-start(bf16[4,8,4096]{2,1,0:T(8,128)(2,1)} %broadcast_in_dim.6), calls=%async_computation | async-start | bytes 524288 | tf_op jit(solution)/shard_map/all_to_all | solution.py:134
  19.5 17.5 %all-to-all-start.1 = ((bf16[4,32,4096]{2,1,0:T(8,128)(2,1)}), bf16[4,32,4096]{2,1,0:T(8,128)(2,1)S(1)}, u32[]{:S(2)}, u32[]{:S(2)}) async-start(bf16[4,32,4096]{2,1,0:T(8,128)(2,1)} %broadcast_in_dim.7), calls=%async_computation.1 | async-start | bytes 2097152 | tf_op jit(solution)/shard_map/all_to_all | solution.py:134

commit v6 on v5

--- a/solution.py
+++ b/solution.py
@@ -102,6 +102,14 @@
         out[:, 128 * half : 128 * half + 128] = total
 
 
+def copy_kernel(held, out, sems):
+    copies = [pltpu.make_async_copy(held, out.at[n], sems.at[n]) for n in range(out.shape[0])]
+    for c in copies:
+        c.start()
+    for c in copies:
+        c.wait()
+
+
 def local(activations, out_grads, projectors, rewards, lengths, pairing, queries):
     tokens, width = activations.shape[1:]
     members = lax.axis_size(PAIR_AXES)
@@ -130,7 +138,19 @@
     held = queries[0]
     gathers = list(PAIR_AXES)
     for stage, axes in enumerate(QUERY_AXES):
-        copies = jnp.broadcast_to(held, (lax.axis_size(axes),) + held.shape)
+        n = lax.axis_size(axes)
+        if stage == 0:
+            copies = jnp.broadcast_to(held, (n,) + held.shape)
+        else:
+            copies = pl.pallas_call(
+                copy_kernel,
+                out_shape=jax.ShapeDtypeStruct((n,) + held.shape, BF16),
+                in_specs=[vmem],
+                out_specs=hbm,
+                scratch_shapes=[pltpu.SemaphoreType.DMA((n,))],
+                compiler_params=pltpu.CompilerParams(vmem_limit_bytes=16 << 20),
+                name="copies",
+            )(held)
         held = lax.all_to_all(copies, axes, 0, 0).reshape(-1, held.shape[1])
         if stage == 0:
             for axis in gathers[:1]:

time: 59.8 us -> 59.7 us (level)
  local copies, waits for them, and re-layouts: 2.62 us -> 1.55 us
  Pallas kernels: 4.17 us -> 5.17 us
    broadcast_in_dim x2 -> x1, local copies, waits for them, and re-layouts: 2.62 us -> 1.55 us  [local(): copies = jnp.broadcast_to(held, (n,) + held.shape)]
    pallas_call x0 -> x1, Pallas kernels: none -> 1 us  [local(): pl.pallas_call(copy_kernel, out_shape=jax.ShapeDtypeStruct((n,) + held.sh...]
where the time goes in v6:
time: 59.7 us; the launch traced here: 59.4 us
  blocking collectives  41.3 us (69%)
  starting transfers between devices  11.4 us (19%)
  Pallas kernels  5.17 us (9%)
  local copies, waits for them, and re-layouts  1.55 us (3%)
    all_to_all x1, blocking collectives, local(): lax.all_to_all(partial.reshape(4 * members, 2, 128), ('layer',) + PAIR_AX...  21.5 us
    all_gather x3, blocking collectives, local(): train = lax.all_gather(train, axis, axis=0, tiled=True)  19.7 us
    all_to_all x2, starting transfers between devices, local(): held = lax.all_to_all(copies, axes, 0, 0).reshape(-1, held.shape[1])  11.4 us
    pallas_call x1, Pallas kernels, local(): pl.pallas_call(train_kernel, out_shape=pltpu.VMEM((16, 512), BF16), in_sp...  3.2 us
    broadcast_in_dim x1, local copies, waits for them, and re-layouts, local(): copies = jnp.broadcast_to(held, (n,) + held.shape)  1.55 us
  transfers between devices with their start and end apart: 2, of which 0 were waited for; matrix products, arithmetic and copies ran while one was open for 0% of the time, Pallas kernels for 5%

profile of v6, /device:TPU:1, one launch (start us, length us, event | category | flops | bytes accessed | tf_op | source)
XLA Modules:
  0.0 59.4 jit_solution(16294019926231079698)
XLA Ops:
  0.0 1.5 %broadcast_in_dim.3 = bf16[4,8,4096]{2,1,0:T(8,128)(2,1)} broadcast(bf16[8,4096]{1,0:T(8,128)(2,1)} %bitcast.9), dimensions={1,2} | broadcast | bytes 327680 | tf_op jit(solution)/shard_map/broadcast_in_dim | solution.py:143
  1.5 7.6 %all-to-all-start = ((bf16[4,8,4096]{2,1,0:T(8,128)(2,1)}), bf16[4,8,4096]{2,1,0:T(8,128)(2,1)S(1)}, u32[]{:S(2)}, u32[]{:S(2)}) async-start(bf16[4,8,4096]{2,1,0:T(8,128)(2,1)} %broadcast_in_dim.3), calls=%async_computation | async-start | bytes 524288 | tf_op jit(solution)/shard_map/all_to_all | solution.py:154
  9.2 3.2 %train.1 = bf16[16,512]{1,0:T(8,128)(2,1)S(1)} custom-call(bf16[1,128,5120]{2,1,0:T(8,128)(2,1)} %act.1, bf16[1,128,5120]{2,1,0:T(8,128)(2,1)} %grad.1, bf16[1,5120,128]{2,1,0:T(8,128)(2,1)} %proj.1, f32[4]{0:T(128)} %rewards_in.1, s32[4]{0:T(128)} %lengths_in.1, s32[2,2]{1,0:T(2,128)} %pairing_in.1), custom_call_target="tpu_custom_call" | custom-call | flops 335544320 | bytes 4194304 | tf_op jit(solution)/shard_map/train/pallas_call | solution.py:119
  12.4 6.0 %all_gather.9 = bf16[32,512]{1,0:T(8,128)(2,1)S(1)} all-gather(bf16[16,512]{1,0:T(8,128)(2,1)S(1)} %train.1), channel_id=1, replica_groups=mesh['layer'=4,'zh'=2,'zm'=2,'zl'=2,'x'=4,'yh'=4] {'zm'}, dimensions={0}, use_global_device_ids=true | all-gather | bytes 49152 | tf_op jit(solution)/shard_map/all_gather | solution.py:157
  18.4 0.0 all-to-all-done
  18.4 1.0 %copies.1 = bf16[4,32,4096]{2,1,0:T(8,128)(2,1)} custom-call(bf16[32,4096]{1,0:T(8,128)(2,1)S(1)} %bitcast.6), custom_call_target="tpu_custom_call" | custom-call | tf_op jit(solution)/shard_map/copies/pallas_call | solution.py:145
  19.4 3.7 %all-to-all-start.1 = ((bf16[4,32,4096]{2,1,0:T(8,128)(2,1)}), bf16[4,32,4096]{2,1,0:T(8,128)(2,1)S(1)}, u32[]{:S(2)}, u32[]{:S(2)}) async-start(bf16[4,32,4096]{2,1,0:T(8,128)(2,1)} %copies.1), calls=%async_computation.1 | async-start | bytes 2097152 | tf_op jit(solution)/shard_map/all_to_all | solution.py:154
  23.1 4.0 %all_gather.10 = bf16[64,512]{1,0:T(8,128)(2,1)S(1)} all-gather(bf16[32,512]{1,0:T(8,128)(2,1)S(1)} %all_gather.9), channel_id=1, replica_groups=mesh['layer'=4,'zh'=2,'zm'=2,'zl'=2,'x'=4,'yh'=4] {'zl'}, dimensions={0}, use_global_device_ids=true | all-gather | bytes 98304 | tf_op jit(solution)/shard_map/all_gather | solution.py:160
  27.2 9.7 %all_gather.11.train = bf16[128,512]{1,0:T(8,128)(2,1)S(1)} all-gather(bf16[64,512]{1,0:T(8,128)(2,1)S(1)} %all_gather.10), channel_id=1, replica_groups=mesh['layer'=4,'zh'=2,'zm'=2,'zl'=2,'x'=4,'yh'=4] {'zh'}, dimensions={0}, use_global_device_ids=true | all-gather | bytes 196608 | tf_op jit(solution)/shard_map/all_gather | solution.py:160
  36.9 0.0 all-to-all-done.1
  36.9 0.4 score.1
  37.2 21.5 %all_to_all.15 = f32[32,2,128]{2,1,0:T(2,128)S(1)} all-to-all(f32[32,2,128]{2,1,0:T(2,128)S(1)} %bitcast.7), channel_id=1, replica_groups=mesh['layer'=4,'zh'=2,'zm'=2,'zl'=2,'x'=4,'yh'=4] {'layer','zh','zl','zm'}, dimensions={0} | all-to-all | bytes 65536 | tf_op jit(solution)/shard_map/all_to_all | solution.py:172
  58.8 0.6 %total.1 = f32[2,256]{1,0:T(2,128)} custom-call(f32[8,2,2,2,128]{4,3,2,1,0:T(2,128)S(1)} %bitcast.8), custom_call_target="tpu_custom_call" | custom-call | tf_op jit(solution)/shard_map/total/pallas_call | solution.py:173
Async XLA Ops:
  1.5 16.8 %all-to-all-start = ((bf16[4,8,4096]{2,1,0:T(8,128)(2,1)}), bf16[4,8,4096]{2,1,0:T(8,128)(2,1)S(1)}, u32[]{:S(2)}, u32[]{:S(2)}) async-start(bf16[4,8,4096]{2,1,0:T(8,128)(2,1)} %broadcast_in_dim.3), calls=%async_computation | async-start | bytes 524288 | tf_op jit(solution)/shard_map/all_to_all | solution.py:154
  19.4 17.5 %all-to-all-start.1 = ((bf16[4,32,4096]{2,1,0:T(8,128)(2,1)}), bf16[4,32,4096]{2,1,0:T(8,128)(2,1)S(1)}, u32[]{:S(2)}, u32[]{:S(2)}) async-start(bf16[4,32,4096]{2,1,0:T(8,128)(2,1)} %copies.1), calls=%async_computation.1 | async-start | bytes 2097152 | tf_op jit(solution)/shard_map/all_to_all | solution.py:154

commit v7 on v5

--- a/solution.py
+++ b/solution.py
@@ -6,7 +6,7 @@
 from jax.sharding import Mesh, PartitionSpec as P
 
 DP = ("zh", "zm", "zl", "x", "yh")
-PAIR_AXES = ("zm", "zl", "zh")
+PAIR_AXES = ("zm", "zh", "zl")
 QUERY_AXES = (("yh",), ("x",))
 CHUNKS = 4
 F32 = jnp.float32
@@ -157,7 +157,7 @@
         out_specs=vmem,
         compiler_params=pltpu.CompilerParams(vmem_limit_bytes=1 << 20),
         name="total",
-    )(got.reshape(-1, 2, 2, 2, 128))
+    )(got.reshape(4, 2, -1, 2, 128))
 
 
 def solution(mesh):

time: 59.8 us -> 59.4 us (level)
    all_to_all x1, blocking collectives: 21.5 us -> 20.9 us  [local(): lax.all_to_all(partial.reshape(4 * members, 2, 128), ('layer',) + PAIR_AX...]
where the time goes in v7:
time: 59.4 us; the launch traced here: 59.1 us
  blocking collectives  40.9 us (69%)
  starting transfers between devices  11.4 us (19%)
  Pallas kernels  4.17 us (7%)
  local copies, waits for them, and re-layouts  2.62 us (4%)
    all_to_all x1, blocking collectives, local(): lax.all_to_all(partial.reshape(4 * members, 2, 128), ('layer',) + PAIR_AX...  20.9 us
    all_gather x3, blocking collectives, local(): train = lax.all_gather(train, axis, axis=0, tiled=True)  20 us
    all_to_all x2, starting transfers between devices, local(): held = lax.all_to_all(copies, axes, 0, 0).reshape(-1, held.shape[1])  11.4 us
    pallas_call x1, Pallas kernels, local(): pl.pallas_call(train_kernel, out_shape=pltpu.VMEM((16, 512), BF16), in_sp...  3.2 us
    broadcast_in_dim x2, local copies, waits for them, and re-layouts, local(): copies = jnp.broadcast_to(held, (lax.axis_size(axes),) + held.shape)  2.62 us
  transfers between devices with their start and end apart: 2, of which 0 were waited for; matrix products, arithmetic and copies ran while one was open for 0% of the time, Pallas kernels for 5%

profile of v7, /device:TPU:1, one launch (start us, length us, event | category | flops | bytes accessed | tf_op | source)
XLA Modules:
  0.0 59.1 jit_solution(6297944316961983666)
XLA Ops:
  0.0 1.5 %broadcast_in_dim.6 = bf16[4,8,4096]{2,1,0:T(8,128)(2,1)} broadcast(bf16[8,4096]{1,0:T(8,128)(2,1)} %bitcast.9), dimensions={1,2} | broadcast | bytes 327680 | tf_op jit(solution)/shard_map/broadcast_in_dim | solution.py:133
  1.5 7.6 %all-to-all-start = ((bf16[4,8,4096]{2,1,0:T(8,128)(2,1)}), bf16[4,8,4096]{2,1,0:T(8,128)(2,1)S(1)}, u32[]{:S(2)}, u32[]{:S(2)}) async-start(bf16[4,8,4096]{2,1,0:T(8,128)(2,1)} %broadcast_in_dim.6), calls=%async_computation | async-start | bytes 524288 | tf_op jit(solution)/shard_map/all_to_all | solution.py:134
  9.2 3.2 %train.1 = bf16[16,512]{1,0:T(8,128)(2,1)S(1)} custom-call(bf16[1,128,5120]{2,1,0:T(8,128)(2,1)} %act.1, bf16[1,128,5120]{2,1,0:T(8,128)(2,1)} %grad.1, bf16[1,5120,128]{2,1,0:T(8,128)(2,1)} %proj.1, f32[4]{0:T(128)} %rewards_in.1, s32[4]{0:T(128)} %lengths_in.1, s32[2,2]{1,0:T(2,128)} %pairing_in.1), custom_call_target="tpu_custom_call" | custom-call | flops 335544320 | bytes 4194304 | tf_op jit(solution)/shard_map/train/pallas_call | solution.py:111
  12.4 6.0 %all_gather.9 = bf16[32,512]{1,0:T(8,128)(2,1)S(1)} all-gather(bf16[16,512]{1,0:T(8,128)(2,1)S(1)} %train.1), channel_id=1, replica_groups=mesh['layer'=4,'zh'=2,'zm'=2,'zl'=2,'x'=4,'yh'=4] {'zm'}, dimensions={0}, use_global_device_ids=true | all-gather | bytes 49152 | tf_op jit(solution)/shard_map/all_gather | solution.py:137
  18.4 0.0 all-to-all-done
  18.4 1.1 %broadcast_in_dim.7 = bf16[4,32,4096]{2,1,0:T(8,128)(2,1)} broadcast(bf16[32,4096]{1,0:T(8,128)(2,1)S(1)} %bitcast.8), dimensions={1,2} | broadcast | bytes 1310720 | tf_op jit(solution)/shard_map/broadcast_in_dim | solution.py:133
  19.5 3.7 %all-to-all-start.1 = ((bf16[4,32,4096]{2,1,0:T(8,128)(2,1)}), bf16[4,32,4096]{2,1,0:T(8,128)(2,1)S(1)}, u32[]{:S(2)}, u32[]{:S(2)}) async-start(bf16[4,32,4096]{2,1,0:T(8,128)(2,1)} %broadcast_in_dim.7), calls=%async_computation.1 | async-start | bytes 2097152 | tf_op jit(solution)/shard_map/all_to_all | solution.py:134
  23.2 9.9 %all_gather.10 = bf16[64,512]{1,0:T(8,128)(2,1)S(1)} all-gather(bf16[32,512]{1,0:T(8,128)(2,1)S(1)} %all_gather.9), channel_id=1, replica_groups=mesh['layer'=4,'zh'=2,'zm'=2,'zl'=2,'x'=4,'yh'=4] {'zh'}, dimensions={0}, use_global_device_ids=true | all-gather | bytes 98304 | tf_op jit(solution)/shard_map/all_gather | solution.py:140
  33.1 4.1 %all_gather.11.train = bf16[128,512]{1,0:T(8,128)(2,1)S(1)} all-gather(bf16[64,512]{1,0:T(8,128)(2,1)S(1)} %all_gather.10), channel_id=1, replica_groups=mesh['layer'=4,'zh'=2,'zm'=2,'zl'=2,'x'=4,'yh'=4] {'zl'}, dimensions={0}, use_global_device_ids=true | all-gather | bytes 196608 | tf_op jit(solution)/shard_map/all_gather | solution.py:140
  37.2 0.0 all-to-all-done.1
  37.2 0.4 score.1
  37.6 20.9 %all_to_all.15 = f32[32,2,128]{2,1,0:T(2,128)S(1)} all-to-all(f32[32,2,128]{2,1,0:T(2,128)S(1)} %bitcast.6), channel_id=1, replica_groups=mesh['layer'=4,'zh'=2,'zm'=2,'zl'=2,'x'=4,'yh'=4] {'layer','zl','zh','zm'}, dimensions={0} | all-to-all | bytes 65536 | tf_op jit(solution)/shard_map/all_to_all | solution.py:152
  58.5 0.6 %total.1 = f32[2,256]{1,0:T(2,128)} custom-call(f32[4,2,4,2,128]{4,3,2,1,0:T(2,128)S(1)} %bitcast.7), custom_call_target="tpu_custom_call" | custom-call | tf_op jit(solution)/shard_map/total/pallas_call | solution.py:153
Async XLA Ops:
  1.5 16.8 %all-to-all-start = ((bf16[4,8,4096]{2,1,0:T(8,128)(2,1)}), bf16[4,8,4096]{2,1,0:T(8,128)(2,1)S(1)}, u32[]{:S(2)}, u32[]{:S(2)}) async-start(bf16[4,8,4096]{2,1,0:T(8,128)(2,1)} %broadcast_in_dim.6), calls=%async_computation | async-start | bytes 524288 | tf_op jit(solution)/shard_map/all_to_all | solution.py:134
  19.5 17.7 %all-to-all-start.1 = ((bf16[4,32,4096]{2,1,0:T(8,128)(2,1)}), bf16[4,32,4096]{2,1,0:T(8,128)(2,1)S(1)}, u32[]{:S(2)}, u32[]{:S(2)}) async-start(bf16[4,32,4096]{2,1,0:T(8,128)(2,1)} %broadcast_in_dim.7), calls=%async_computation.1 | async-start | bytes 2097152 | tf_op jit(solution)/shard_map/all_to_all | solution.py:134
